TPU v7x, 512 devices: a whole 4x4x16 slice. The times are simulated.
512 devices in a mesh: ctx: 64 (over x, z_lo, core), tp: 8 (over z_hi, y).
Axes of the slice: x: 4, y: 4, z: 16 (z_hi: 2, z_lo: 8; z = z_hi * 8 + z_lo), core: 2. Of those that a mesh axis runs over, the one named last changes fastest.
Arguments:
- tokens: bfloat16 [8192, 4096], P('ctx', 'tp'), may hold values from -6 to 6
- w_in: bfloat16 [4096, 3, 512], P('tp'), may hold values from -0.09375 to 0.09375
- grad_out: bfloat16 [8192, 512], P('ctx', 'tp'), may hold values from -6 to 6
- filters: float32 [8, 64, 8192], P('tp', 'ctx'), may hold values from -2 to 2
Outputs:
- input_grad: bfloat16 [8192, 4096], P('ctx', 'tp')
- weight_grad: float32 [512, 3, 4096], P('ctx', None, 'tp')
- filter_grad: float32 [8, 64, 8192], P('tp', 'ctx')
All inputs are finite; a program needn't handle non-finite values.
Results may differ from a plain program's by a relative error of at most 0.025.
Values may be sent and summed in bfloat16 or wider, within the bound.
A program may use at most 64 MiB of HBM per device.

v0:
```python
import math

import jax
import jax.numpy as jnp
from jax import lax
from jax.sharding import PartitionSpec as P


def matmul_high(left, right):
    return jnp.matmul(left, right, precision=lax.Precision.HIGHEST)


def table(size, sign):
    index = jnp.arange(size, dtype=jnp.int32)
    phase = index[:, None] * index[None, :] % size
    angle = phase.astype(jnp.float32) * (sign * 2.0 * math.pi / size)
    return (jnp.cos(angle), jnp.sin(angle))


def fourier(real_part, imag_part, sign):
    size = real_part.shape[-1]
    if size <= 128 or size % 64 != 0:
        cosine, sine = table(size, sign)
        out_real = matmul_high(real_part, cosine) - matmul_high(imag_part, sine)
        out_imag = matmul_high(real_part, sine) + matmul_high(imag_part, cosine)
        return (out_real, out_imag)
    outer = 64
    inner = size // outer
    lead = real_part.shape[:-1]
    grid_real = real_part.reshape(lead + (outer, inner))
    grid_imag = imag_part.reshape(lead + (outer, inner))
    cosine, sine = table(outer, sign)

    def apply(matrix, grid):
        return jnp.einsum("ak,...an->...kn", matrix, grid, precision=lax.Precision.HIGHEST)

    first_real = apply(cosine, grid_real) - apply(sine, grid_imag)
    first_imag = apply(sine, grid_real) + apply(cosine, grid_imag)
    rows = jnp.arange(outer, dtype=jnp.int32)[:, None]
    cols = jnp.arange(inner, dtype=jnp.int32)[None, :]
    angle = (rows * cols).astype(jnp.float32) * (sign * 2.0 * math.pi / size)
    twist_cos, twist_sin = (jnp.cos(angle), jnp.sin(angle))
    turned_real = first_real * twist_cos - first_imag * twist_sin
    turned_imag = first_real * twist_sin + first_imag * twist_cos
    last_real, last_imag = fourier(turned_real, turned_imag, sign)
    out_real = jnp.swapaxes(last_real, -1, -2).reshape(lead + (size,))
    out_imag = jnp.swapaxes(last_imag, -1, -2).reshape(lead + (size,))
    return (out_real, out_imag)


def on_device(tokens, w_in, grad_out, filters):
    summed = lax.psum_scatter(
        jnp.einsum("ra,ajc->cjr", tokens, w_in, preferred_element_type=jnp.float32).astype(
            jnp.bfloat16
        ),
        "tp",
        scatter_dimension=0,
        tiled=True,
    )
    packed = jnp.stack([summed[:, 0], summed[:, 1], summed[:, 2], grad_out.T])
    channels = lax.all_to_all(packed, "ctx", split_axis=1, concat_axis=2, tiled=True)
    length = channels.shape[2]
    query = channels[0].astype(jnp.float32)
    key_part = channels[1].astype(jnp.float32)
    value = channels[2].astype(jnp.float32)
    cotangent = channels[3].astype(jnp.float32)
    mixed = key_part * value
    grad_y = cotangent * query
    stacked = jnp.stack([mixed, filters[0], grad_y])
    stacked = jnp.pad(stacked, ((0, 0), (0, 0), (0, length)))
    spec_real, spec_imag = fourier(stacked, jnp.zeros_like(stacked), -1.0)
    mix_r, filt_r, grad_r = (spec_real[0], spec_real[1], spec_real[2])
    mix_i, filt_i, grad_i = (spec_imag[0], spec_imag[1], spec_imag[2])
    prod_real = jnp.stack(
        [
            filt_r * mix_r - filt_i * mix_i,
            filt_r * grad_r + filt_i * grad_i,
            mix_r * grad_r + mix_i * grad_i,
        ]
    )
    prod_imag = jnp.stack(
        [
            filt_r * mix_i + filt_i * mix_r,
            filt_r * grad_i - filt_i * grad_r,
            mix_r * grad_i - mix_i * grad_r,
        ]
    )
    back_real, back_imag = fourier(prod_real, prod_imag, 1.0)
    results = back_real[:, :, :length] / (2.0 * length)
    output = results[0]
    grad_query = (cotangent * output).astype(jnp.bfloat16)
    grad_mixed = results[1].astype(jnp.bfloat16)
    filter_grad = (results[2] / math.sqrt(length))[None]
    grad_key = (grad_mixed.astype(jnp.float32) * value).astype(jnp.bfloat16)
    grad_value = (grad_mixed.astype(jnp.float32) * key_part).astype(jnp.bfloat16)
    returned = lax.all_to_all(
        jnp.stack([grad_query, grad_key, grad_value]),
        "ctx",
        split_axis=2,
        concat_axis=1,
        tiled=True,
    )
    whole = lax.all_gather(returned, "tp", axis=1, tiled=True)
    scale = 1.0 / math.sqrt(length)
    term = jnp.einsum("jcr,ra->cja", whole, tokens, preferred_element_type=jnp.float32)
    weight_grad = lax.psum_scatter(term * scale, "ctx", scatter_dimension=0, tiled=True)
    input_grad = jnp.einsum("jcr,ajc->ra", whole, w_in, preferred_element_type=jnp.float32).astype(
        jnp.bfloat16
    )
    return (input_grad, weight_grad, filter_grad)


def solution(mesh):
    placed = (P("ctx", "tp"), P("tp", None, None), P("ctx", "tp"), P("tp", "ctx", None))
    return jax.shard_map(
        on_device,
        mesh=mesh,
        in_specs=placed,
        out_specs=(P("ctx", "tp"), P("ctx", None, "tp"), P("tp", "ctx", None)),
        check_vma=False,
    )
```

profile of v0, /device:TPU:24, one launch (start us, length us, event | category | flops | bytes accessed | tf_op | source)
XLA Modules:
  0.0 768.2 jit_solution(6455832966753837880)
XLA Ops:
  7.2 1.3 copy-done
  8.6 2.3 fusion
  10.9 116.4 %reduce-scatter.3.cloned.1.call-done = bf16[64,3,128]{2,0,1:T(8,128)(2,1)} async-done(((bf16[512,3,128]{2,0,1:T(8,128)(2,1)}), bf16[64,3,128]{2,0,1:T(8,128)(2,1)}) %reduce-scatter.3.cloned.1.call-update) | async-done | bytes 49168 | tf_op jit(solution)/shard_map/reduce_scatter | solution.py:52
  127.3 0.8 slice_bitcast_fusion.6
  128.7 5.7 all-to-all-start
  135.1 12.2 %all-to-all-done = bf16[4,64,128]{2,0,1:T(4,128)(2,1)S(1)} async-done(((bf16[4,64,128]{2,0,1:T(4,128)(2,1)}), bf16[4,64,128]{2,0,1:T(4,128)(2,1)S(1)}, u32[]{:S(2)}, u32[]{:S(2)}) %all-to-all-start) | async-done | bytes 65568 | tf_op jit(solution)/shard_map/all_to_all | solution.py:61
  152.7 1.0 fusion.18
  153.8 1.0 fusion.20
  154.8 1.0 fusion.5
  155.9 1.0 fusion.4
  160.4 0.8 fusion.51
  163.4 1.0 fusion.14
  164.4 1.0 fusion.1
  166.0 0.8 fusion.42
  166.9 6.8 copy.185
  174.2 46.5 %reduce.2 = bf16[8192,3]{1,0:T(8,128)(2,1)} reduce(bf16[8192,1,3]{2,1,0:T(2,128)(2,1)} %bitcast.265, bf16[]{:T(256)} %broadcast.302), dimensions={1}, to_apply=%bitcast.236.reduce_sub_computation | reduce | bytes 98306
  220.8 4.2 reshape.732
  225.0 17.7 %all_to_all.21 = bf16[64,2,192]{2,1,0:T(2,128)(2,1)S(1)} all-to-all(bf16[64,2,192]{2,1,0:T(2,128)(2,1)S(1)} %reshape.732), channel_id=1, replica_groups=mesh['ctx'=64,'tp'=8] {'ctx'}, dimensions={0} | all-to-all | bytes 98304 | tf_op jit(solution)/shard_map/all_to_all | solution.py:96
  242.6 8.3 %reshape.733 = bf16[8192,1,3]{2,1,0:T(2,128)(2,1)} reshape(bf16[64,2,192]{2,1,0:T(2,128)(2,1)S(1)} %all_to_all.21) | data formatting | bytes 98304
  250.9 8.1 %copy.186 = bf16[3,1,8192]{2,0,1:T(4,128)(2,1)S(1)} copy(bf16[3,1,8192]{0,1,2:T(2,128)(2,1)} %bitcast.266) | data formatting | bytes 98304 | tf_op jit(solution)/shard_map/all_to_all | solution.py:96
  259.1 63.9 %all_gather.3 = bf16[3,512,128]{2,1,0:T(8,128)(2,1)S(1)} all-gather(bf16[3,64,128]{2,1,0:T(8,128)(2,1)S(1)} %bitcast.291), channel_id=1, replica_groups=mesh['ctx'=64,'tp'=8] {'tp'}, dimensions={1}, use_global_device_ids=true | all-gather | bytes 442368 | tf_op jit(solution)/shard_map/all_gather | solution.py:103
  323.0 2.2 multiply_bitcast_fusion
  325.2 1.3 fusion.12
  326.5 434.8 %reduce-scatter.5.cloned.1.call-done = f32[8,3,512]{2,0,1:T(8,128)} async-done(((f32[512,3,512]{2,0,1:T(8,128)}), f32[8,3,512]{2,0,1:T(8,128)}) %reduce-scatter.5.cloned.1.call-update) | async-done | bytes 49168 | tf_op jit(solution)/shard_map/reduce_scatter | solution.py:106
  (58 shorter events, 13.5 us)
Async XLA Ops:
  7.2 1.4 copy-start
  7.2 120.9 %copy-start.3 = (bf16[128,64]{0,1:T(8,128)(2,1)S(1)}, bf16[128,64]{0,1:T(8,128)(2,1)}, u32[]{:S(2)}) copy-start(bf16[128,64]{0,1:T(8,128)(2,1)} %param.6) | copy-start | bytes 49156
  7.2 140.1 %copy-start.2 = (f32[1,1,8192]{2,1,0:T(1,128)S(1)}, f32[1,1,8192]{2,1,0:T(1,128)}, u32[]{:S(2)}) copy-start(f32[1,1,8192]{2,1,0:T(1,128)} %param.7) | copy-start | bytes 98308
  7.2 120.1 %reduce-scatter.3.cloned.1.call-start = ((), (), s32[]{:S(2)}) async-start(), calls=%async_computation.4 | async-start | bytes 442368 | tf_op jit(solution)/shard_map/reduce_scatter | solution.py:52
  128.7 18.5 %all-to-all-start = ((bf16[4,64,128]{2,0,1:T(4,128)(2,1)}), bf16[4,64,128]{2,0,1:T(4,128)(2,1)S(1)}, u32[]{:S(2)}, u32[]{:S(2)}) async-start(bf16[4,64,128]{2,0,1:T(4,128)(2,1)} %copy.149), calls=%async_computation.1 | async-start | bytes 131072 | tf_op jit(solution)/shard_map/all_to_all | solution.py:61
  134.5 626.9 %reduce-scatter.5.cloned.1.call-start = ((), (), s32[]{:S(2)}) async-start(), calls=%async_computation.5 | async-start | bytes 3194880 | tf_op jit(solution)/shard_map/reduce_scatter | solution.py:106
  250.9 72.0 %copy-start.1 = (bf16[128,512]{1,0:T(8,128)(2,1)S(1)}, bf16[128,512]{1,0:T(8,128)(2,1)}, u32[]{:S(2)}) copy-start(bf16[128,512]{1,0:T(8,128)(2,1)} %param.4) | copy-start | bytes 393220
Sparse Core Ops, SparseCore 0:
  12.5 114.7 reduce-scatter.2
  325.3 435.9 reduce-scatter.4
where the time goes:
time: 769 us; the launch traced here: 768 us
  waiting for transfers between devices  563 us (73%)
  blocking collectives  81.5 us (11%)
  other arithmetic  48.7 us (6%)
  local copies, waits for them, and re-layouts  33.4 us (4%)
  matrix products  20.9 us (3%)
  between operations  14.4 us (2%)
    reduce_scatter x1, waiting for transfers between devices, on_device(): lax.psum_scatter(term * scale, 'ctx', scatter_dimension=0, tiled=True)  435 us
    reduce_scatter x1, waiting for transfers between devices, on_device(): lax.psum_scatter(jnp.einsum('ra,ajc->cjr', tokens, w_in, preferred_elemen...  116 us
    all_gather x1, blocking collectives, on_device(): whole = lax.all_gather(returned, 'tp', axis=1, tiled=True)  63.9 us
    unnamed x1, other arithmetic  46.5 us
    all_to_all x1, blocking collectives, on_device(): lax.all_to_all(jnp.stack([grad_query, grad_key, grad_value]), 'ctx', spli...  17.7 us
  transfers between devices with their start and end apart: 3, of which 3 were waited for; matrix products, arithmetic and copies ran while one was open for 0% of the time, Pallas kernels for 0%

commit v1 on v0

v1 whole, which is shorter than its diff:
```python
import math

import jax
import jax.numpy as jnp
import numpy as np
from jax import lax
from jax.experimental import pallas as pl
from jax.experimental.pallas import tpu as pltpu
from jax.sharding import PartitionSpec as P

LENGTH = 8192
POINTS = 2 * LENGTH
MESH = pl.DeviceIdType.MESH
F32, BF16 = jnp.float32, jnp.bfloat16
EXACT = lax.Precision.HIGHEST


def selection(outs, ins, pairs):
    matrix = np.zeros((outs, ins), np.float32)
    for row, column in pairs:
        matrix[row, column] = 1.0
    return matrix


def selections():
    def ctx(p, zl):
        return (p >> 1) * 16 + zl * 2 + (p & 1)

    eight = range(8)
    r2q = selection(256, 192, [(zl * 32 + i * 8 + p, i * 64 + ctx(p, zl)) for zl in eight for i in range(3) for p in eight])
    r2g = selection(256, 64, [(zl * 32 + 24 + p, ctx(p, zl)) for zl in eight for p in eight])
    r3 = selection(
        256,
        512,
        [(p * 32 + i * 8 + zl, zh * 256 + zl * 32 + i * 8 + p) for zh in range(2) for zl in eight for i in range(4) for p in eight],
    )
    r5 = selection(256, 192, [(zl * 32 + i * 8 + p, i * 64 + p * 8 + zl) for zl in eight for i in range(3) for p in eight])
    r6 = selection(384, 512, [(p * 48 + z * 3 + i, z * 32 + i * 8 + p) for z in range(16) for i in range(3) for p in eight])
    r8 = selection(192, 192, [(m * 48 + q * 12 + r, q * 48 + m * 12 + r) for m in range(4) for q in range(4) for r in range(12)])
    r9 = selection(
        384,
        384,
        [(i * 128 + zh * 64 + ctx(p, zl), p * 48 + zh * 24 + zl * 3 + i) for i in range(3) for zh in range(2) for zl in eight for p in eight],
    )
    return [m.astype(jnp.bfloat16) for m in (r2q, r2g, r3, r5, r6, r8, r9)]


def transforms():
    turn = 2.0 * math.pi
    natural = np.arange(64)
    moved = np.array([(p >> 1) * 16 + zl * 2 + (p & 1) for p in range(8) for zl in range(8)])
    k = np.arange(128)

    def first(rows):
        angle = turn * ((k[:, None] * rows[None, :]) % 128) / 128
        return np.concatenate([np.cos(angle), -np.sin(angle)], 0)

    def last(rows, scale):
        angle = turn * ((rows[:, None] * k[None, :]) % 128) / 128
        return np.concatenate([np.cos(angle), -np.sin(angle)], 1) * scale

    angle = turn * (k[:, None] * k[None, :]) / POINTS
    twist = (np.cos(angle), -np.sin(angle))
    angle = turn * ((k[:, None] * k[None, :]) % 128) / 128
    c, s = np.cos(angle), np.sin(angle)
    forward = np.block([[c, -s], [s, c]])
    back = np.block([[c, s], [-s, c]])
    tables = (
        first(moved),
        first(natural),
        *twist,
        forward,
        back,
        last(moved, 1.0 / POINTS),
        last(natural, 1.0 / (POINTS * math.sqrt(LENGTH))),
    )
    return [t.astype(np.float32) for t in tables]


def dot(left, right, precision=None):
    return jnp.dot(left, right, precision=precision, preferred_element_type=F32)


def kernel(
    tok, w, go, filt,
    r2q, r2g, r3, r5, r6, r8, r9,
    f1p, f1n, twr, twi, mf, mi, g1p, g1n,
    ig_out, wg_out, fg_out,
    part, recv1, send2, recv2, send3, recv3, send5, recv5, recv6, recv7, send8, recv8, toks, gnat,
    s1, t1, s2, t2, s3, t3, s5, t5, s6, t6, s7, t7, s8, t8, sx, tx, sc, tc,
):
    k, j = lax.axis_index("ctx"), lax.axis_index("tp")
    x, zl, core = k // 16, (k // 2) % 8, k % 2
    zh, y = j // 4, j % 4
    z, p = zh * 8 + zl, x * 2 + core

    def at(x_, zl_, core_, zh_, y_):
        return (x_ * 16 + zl_ * 2 + core_, zh_ * 4 + y_)

    def at_y(y_):
        return at(x, zl, core, zh, y_)

    def at_z(z_):
        return at(x, z_ % 8, core, z_ // 8, y)

    def at_p(p_):
        return at(p_ // 2, zl, p_ % 2, zh, y)

    def target8(m):
        return at(((m // 2) % 2) * 2 + m // 8, ((m // 4) % 2) * 4 + x, m % 2, zh, y)

    def source8(s):
        return at(zl % 4, s % 8, s // 8, zh, y)

    own8 = zl % 4 == x
    own_m = ((x % 2) * 2 + zl // 4) * 4 + (x // 2) * 2 + core

    def each(low, high, body):
        def step(n, carry):
            body(n)
            return carry

        lax.fori_loop(low, high, step, 0)

    def send(src, dst, s, t, to):
        pltpu.make_async_remote_copy(
            src_ref=src, dst_ref=dst, send_sem=s, recv_sem=t, device_id=to, device_id_type=MESH
        ).start()

    def take(ref, sem):
        pltpu.make_async_copy(ref, ref, sem).wait()

    barrier = pltpu.get_barrier_semaphore()

    def greet(to):
        pl.semaphore_signal(barrier, inc=1, device_id=to, device_id_type=MESH)

    each(1, 4, lambda n: greet(at_y((y + n) % 4)))
    each(1, 16, lambda n: greet(at_z((z + n) % 16)))
    each(1, 8, lambda n: greet(at_p((p + n) % 8)))

    def greet8(s):
        @pl.when(jnp.logical_not(jnp.logical_and(own8, s == core * 8 + zl)))
        def _():
            greet(source8(s))

    each(0, 16, greet8)

    for i in range(3):
        rows = dot(tok[...], w[i]).T.astype(BF16)
        for h in range(2):
            for yy in range(4):
                first = (h * 4 + yy) * 64
                part[yy, i * 128 + h * 64 : i * 128 + h * 64 + 64, :] = rows[first : first + 64]
    toks[p] = tok[...]

    pl.semaphore_wait(barrier, 25 + jnp.where(own8, 15, 16))

    for n in range(1, 4):
        to = (y + n) % 4
        send(part.at[to], recv1.at[n - 1], s1, t1, at_y(to))
    each(1, 4, lambda n: send(tok, toks.at[p], sx, tx, at_p((p + 2 * n) % 8)))
    sibling = x * 2 + (1 - core)
    send(tok, toks.at[p], sc, tc, at_p(sibling))

    twist_r, twist_i = twr[...], twi[...]

    def spectrum(table, rows, count):
        a = dot(table[...], rows, EXACT)
        ar, ai = a[:128], a[128:]
        pieces = []
        for n in range(count):
            br, bi = ar[:, n * 128 : n * 128 + 128], ai[:, n * 128 : n * 128 + 128]
            pieces.append(jnp.concatenate([br * twist_r - bi * twist_i, br * twist_i + bi * twist_r], axis=1))
        return dot(jnp.concatenate(pieces, axis=0), mf[...], EXACT)

    def inverse(spectra):
        d = dot(jnp.concatenate(spectra, axis=0), mi[...], EXACT)
        reals, imags = [], []
        for n in range(len(spectra)):
            dr, di = d[n * 128 : n * 128 + 128, :128], d[n * 128 : n * 128 + 128, 128:]
            reals.append(dr * twist_r + di * twist_i)
            imags.append(di * twist_r - dr * twist_i)
        return jnp.concatenate([jnp.concatenate(reals, axis=1), jnp.concatenate(imags, axis=1)], axis=0)

    filt_f = spectrum(f1n, filt[...], 1)
    filt_r, filt_i = filt_f[:, :128], filt_f[:, 128:]
    cotangent = dot(r2g[...], go[...])

    take(recv1, t1)
    total = part[y].astype(F32)
    for n in range(3):
        total = total + recv1[n].astype(F32)
    total = total.astype(BF16)
    for h in range(2):
        rows = jnp.concatenate([total[i * 128 + h * 64 : i * 128 + h * 64 + 64] for i in range(3)], axis=0)
        moved = dot(r2q[...], rows) + cotangent * jnp.where(zh == h, 1.0, 0.0)
        send2[h * 8 : h * 8 + 8] = moved.astype(BF16).reshape(8, 32, 128)

    def to_z(buffer, dst, s, t, slab):
        def body(n):
            to = (z + n) % 16
            send(buffer.at[slab(to)], dst.at[z], s, t, at_z(to))

        each(1, 16, body)

    to_z(send2, recv2, s2, t2, lambda to: to)
    recv2[z] = send2[z]

    take(toks.at[pl.ds(0, 3)], tx)

    def forward(n):
        block = (p + 2 * n) % 8
        send(toks.at[block], toks.at[block], sc, tc, at_p(sibling))

    each(1, 4, forward)

    take(recv2.at[pl.ds(0, 15)], t2)
    moved = dot(r3[...], recv2[...].reshape(512, 128))
    send3[...] = moved.astype(BF16).reshape(8, 32, 128)

    def to_p3(n):
        to = (p + n) % 8
        send(send3.at[to], recv3.at[p], s3, t3, at_p(to))

    each(1, 8, to_p3)
    recv3[p] = send3[p]
    take(recv3.at[pl.ds(0, 7)], t3)

    lines = recv3[...].astype(F32).reshape(8, 4, 8, 128)
    query, key_part, value, cot = [lines[:, i].reshape(64, 128) for i in range(4)]
    spectra = spectrum(f1p, jnp.concatenate([key_part * value, cot * query], axis=1), 2)
    mix_r, mix_i = spectra[:128, :128], spectra[:128, 128:]
    grad_r, grad_i = spectra[128:, :128], spectra[128:, 128:]
    out_f = jnp.concatenate([filt_r * mix_r - filt_i * mix_i, filt_r * mix_i + filt_i * mix_r], axis=1)
    back_f = jnp.concatenate([filt_r * grad_r + filt_i * grad_i, filt_r * grad_i - filt_i * grad_r], axis=1)
    both = dot(g1p[...], inverse([out_f, back_f]), EXACT)
    grad_query = (cot * both[:, :128]).astype(BF16)
    grad_mixed = both[:, 128:].astype(BF16).astype(F32)
    grad_key = (grad_mixed * value).astype(BF16)
    grad_value = (grad_mixed * key_part).astype(BF16)

    rows = jnp.concatenate([grad_query, grad_key, grad_value], axis=0)
    send5[...] = dot(r5[...], rows).astype(BF16).reshape(8, 32, 128)
    to_z(send5, recv5, s5, t5, lambda to: to % 8)
    recv5[z] = send5[zl]

    filt_f = jnp.concatenate([mix_r * grad_r + mix_i * grad_i, mix_r * grad_i - mix_i * grad_r], axis=1)
    fg_out[...] = dot(g1n[...], inverse([filt_f]), EXACT)

    take(recv5.at[pl.ds(0, 15)], t5)
    moved = dot(r6[...], recv5[...].reshape(512, 128))
    recv6[y] = moved.astype(BF16).reshape(8, 48, 128)
    for n in range(1, 4):
        send(recv6.at[y], recv6.at[y], s6, t6.at[4 - n], at_y((y + n) % 4))

    take(toks.at[pl.ds(0, 4)], tc)
    for n in range(4):
        yy = (y + n) % 4
        if n > 0:
            take(recv6.at[yy], t6.at[n])

        def to_p7(r, yy=yy):
            to = (p + r) % 8
            send(recv6.at[yy, to], recv7.at[p, yy], s7, t7, at_p(to))

        each(1, 8, to_p7)
        recv7[p, yy] = recv6[yy, p]
        wide = jnp.concatenate([recv6[yy, b] for b in range(8)], axis=1)
        term = dot(wide, toks[...].reshape(1024, 512)).astype(BF16)
        tall = jnp.concatenate([term[:, q * 128 : q * 128 + 128] for q in range(4)], axis=0)
        send8[pl.ds(yy * 4, 4)] = dot(r8[...], tall).astype(BF16).reshape(4, 48, 128)

        def to_8(r, yy=yy):
            m = yy * 4 + r
            mine = jnp.logical_and(own8, m == own_m)

            @pl.when(mine)
            def _():
                pltpu.make_async_copy(send8.at[m], recv8.at[core * 8 + zl], t8).start()

            @pl.when(jnp.logical_not(mine))
            def _():
                send(send8.at[m], recv8.at[core * 8 + zl], s8, t8, target8(m))

        each(0, 4, to_8)

    take(recv7.at[pl.ds(0, 7)], t7)
    for yy in range(4):
        rows = recv7[:, yy].reshape(384, 128)
        moved = dot(r9[...], rows).astype(BF16)
        for i in range(3):
            for h in range(2):
                gnat[i, (h * 4 + yy) * 64 : (h * 4 + yy) * 64 + 64, :] = moved[i * 128 + h * 64 : i * 128 + h * 64 + 64]
    turned = dot(w[0], gnat[0]) + dot(w[1], gnat[1]) + dot(w[2], gnat[2])
    ig_out[...] = turned.T.astype(BF16)

    take(recv8, t8)
    for c in range(2):
        total = recv8[c * 8].astype(F32)
        for n in range(1, 8):
            total = total + recv8[c * 8 + n].astype(F32)
        total = total * (1.0 / math.sqrt(LENGTH))
        for r in range(4):
            for q in range(4):
                wg_out[r * 2 + c, :, q * 128 : q * 128 + 128] = total[q * 12 + r * 3 : q * 12 + r * 3 + 3]

    take(recv1, s1)
    take(recv2.at[pl.ds(0, 15)], s2)
    take(recv3.at[pl.ds(0, 7)], s3)
    take(recv5.at[pl.ds(0, 15)], s5)
    take(recv6.at[pl.ds(0, 3)], s6)
    take(recv7.at[pl.ds(0, 7)], s7)
    take(toks.at[pl.ds(0, 3)], sx)
    take(toks.at[pl.ds(0, 4)], sc)
    take(recv8.at[pl.ds(0, 15)], s8)

    @pl.when(jnp.logical_not(own8))
    def _():
        take(recv8.at[0], s8)


def on_device(tokens, w_in, grad_out, filters):
    tables = [jnp.asarray(t) for t in selections()] + [jnp.asarray(t) for t in transforms()]
    vmem = pl.BlockSpec(memory_space=pltpu.VMEM)
    dma = pltpu.SemaphoreType.DMA
    input_grad, weight_grad, filter_grad = pl.pallas_call(
        kernel,
        out_shape=(
            jax.ShapeDtypeStruct((128, 512), BF16),
            jax.ShapeDtypeStruct((8, 3, 512), F32),
            jax.ShapeDtypeStruct((64, 128), F32),
        ),
        in_specs=[vmem] * (4 + len(tables)),
        out_specs=(vmem, vmem, vmem),
        scratch_shapes=[
            pltpu.VMEM((4, 384, 128), BF16),
            pltpu.VMEM((3, 384, 128), BF16),
            pltpu.VMEM((16, 32, 128), BF16),
            pltpu.VMEM((16, 32, 128), BF16),
            pltpu.VMEM((8, 32, 128), BF16),
            pltpu.VMEM((8, 32, 128), BF16),
            pltpu.VMEM((8, 32, 128), BF16),
            pltpu.VMEM((16, 32, 128), BF16),
            pltpu.VMEM((4, 8, 48, 128), BF16),
            pltpu.VMEM((8, 4, 48, 128), BF16),
            pltpu.VMEM((16, 48, 128), BF16),
            pltpu.VMEM((16, 48, 128), BF16),
            pltpu.VMEM((8, 128, 512), BF16),
            pltpu.VMEM((3, 512, 128), BF16),
            dma, dma, dma, dma, dma, dma, dma, dma,
            dma, dma((4,)),
            dma, dma, dma, dma, dma, dma, dma, dma,
        ],
        compiler_params=pltpu.CompilerParams(collective_id=0, has_side_effects=True, vmem_limit_bytes=40 * 1024 * 1024),
    )(tokens, w_in.transpose(1, 0, 2), grad_out.T, filters.reshape(64, 128), *tables)
    return input_grad, weight_grad, filter_grad.reshape(1, 1, LENGTH)


def solution(mesh):
    placed = (P("ctx", "tp"), P("tp", None, None), P("ctx", "tp"), P("tp", "ctx", None))
    return jax.shard_map(
        on_device,
        mesh=mesh,
        in_specs=placed,
        out_specs=(P("ctx", "tp"), P("ctx", None, "tp"), P("tp", "ctx", None)),
        check_vma=False,
    )
```

time: 769 us -> 91.2 us (0.12)
  the two profiles are of different devices: /device:TPU:24 before, /device:TPU:31 now
where the time goes in v1:
time: 91.2 us; the launch traced here: 90.4 us
  Pallas kernels  70.5 us (77%)
  local copies, waits for them, and re-layouts  19.2 us (21%)
    pallas_call x1, Pallas kernels, on_device(): pl.pallas_call(kernel, out_shape=(jax.ShapeDtypeStruct((128, 512), BF16),...  70.5 us
    unnamed x41, local copies, waits for them, and re-layouts  19.2 us

profile of v1, /device:TPU:31, one launch (start us, length us, event | category | flops | bytes accessed | tf_op | source)
XLA Modules:
  0.0 90.4 jit_solution(2183737414745197094)
XLA Ops:
  0.6 0.0 copy-start
  0.6 1.4 %copy-done = bf16[512,3,512]{2,0,1:T(8,128)(2,1)S(1)} copy-done((bf16[512,3,512]{2,0,1:T(8,128)(2,1)S(1)}, bf16[512,3,512]{2,0,1:T(8,128)(2,1)}, u32[]{:S(2)}) %copy-start) | copy-done | bytes 1572888
  2.0 1.0 %copy-done.1 = bf16[384,512]{1,0:T(8,128)(2,1)S(1)} copy-done((bf16[384,512]{1,0:T(8,128)(2,1)S(1)}, bf16[384,512]{1,0:T(8,128)(2,1)}, u32[]{:S(2)}) %copy-start.1) | copy-done | bytes 393240
  3.0 1.0 %copy-done.2 = bf16[384,384]{1,0:T(8,128)(2,1)S(1)} copy-done((bf16[384,384]{1,0:T(8,128)(2,1)S(1)}, bf16[384,384]{1,0:T(8,128)(2,1)}, u32[]{:S(2)}) %copy-start.2) | copy-done | bytes 294936
  4.0 0.9 %copy-done.3 = f32[256,256]{1,0:T(8,128)S(1)} copy-done((f32[256,256]{1,0:T(8,128)S(1)}, f32[256,256]{1,0:T(8,128)}, u32[]{:S(2)}) %copy-start.3) | copy-done | bytes 262168
  5.0 0.9 %copy-done.4 = f32[256,256]{1,0:T(8,128)S(1)} copy-done((f32[256,256]{1,0:T(8,128)S(1)}, f32[256,256]{1,0:T(8,128)}, u32[]{:S(2)}) %copy-start.4) | copy-done | bytes 262168
  5.9 0.9 %copy-done.5 = bf16[256,512]{1,0:T(8,128)(2,1)S(1)} copy-done((bf16[256,512]{1,0:T(8,128)(2,1)S(1)}, bf16[256,512]{1,0:T(8,128)(2,1)}, u32[]{:S(2)}) %copy-start.5) | copy-done | bytes 262168
  6.9 0.9 copy-done.6
  7.8 0.9 copy-done.7
  8.7 0.9 copy-done.8
  9.6 0.9 copy-done.9
  10.5 0.9 copy-done.10
  11.4 0.9 copy-done.11
  12.3 0.8 copy-done.12
  13.1 0.8 copy-done.13
  13.9 0.8 copy-done.14
  14.8 0.8 copy-done.15
  15.6 0.8 copy-done.16
  16.5 0.8 copy-done.17
  17.2 0.7 copy-done.18
  17.9 70.5 %shard_map.202 = (bf16[128,512]{1,0:T(8,128)(2,1)S(1)}, f32[8,3,512]{2,1,0:T(4,128)S(1)}, f32[64,128]{1,0:T(8,128)S(1)}) custom-call(bf16[128,512]{1,0:T(8,128)(2,1)S(1)} %copy-done.6, bf16[3,512,512]{2,1,0:T(8,128)(2,1)S(1)} %bitcast.4, bf16[64,128]{1,0:T(8,128)(2,1)S(1)} %bitcast.7, f32[64,128]{1,0:T(8,128)S(1)} %bitcast.5, ...), custom_call_target="tpu_custom_call" | custom-call | tf_op jit(solution)/shard_map/pallas_call | solution.py:327
  88.5 0.6 copy.22
  89.1 0.7 copy.25
  89.8 0.6 copy.26
  (18 shorter events, 0.0 us)
Async XLA Ops:
  0.6 1.4 %copy-start = (bf16[512,3,512]{2,0,1:T(8,128)(2,1)S(1)}, bf16[512,3,512]{2,0,1:T(8,128)(2,1)}, u32[]{:S(2)}) copy-start(bf16[512,3,512]{2,0,1:T(8,128)(2,1)} %param.20) | copy-start | bytes 4718596
  2.0 1.0 %copy-start.1 = (bf16[384,512]{1,0:T(8,128)(2,1)S(1)}, bf16[384,512]{1,0:T(8,128)(2,1)}, u32[]{:S(2)}) copy-start(bf16[384,512]{1,0:T(8,128)(2,1)} %constant.34.clone.r6) | copy-start | bytes 1179652
  3.0 1.0 %copy-start.2 = (bf16[384,384]{1,0:T(8,128)(2,1)S(1)}, bf16[384,384]{1,0:T(8,128)(2,1)}, u32[]{:S(2)}) copy-start(bf16[384,384]{1,0:T(8,128)(2,1)} %constant.36.clone.r9) | copy-start | bytes 884740
  4.0 0.9 %copy-start.3 = (f32[256,256]{1,0:T(8,128)S(1)}, f32[256,256]{1,0:T(8,128)}, u32[]{:S(2)}) copy-start(f32[256,256]{1,0:T(8,128)} %constant.42.clone.mi) | copy-start | bytes 786436
  4.9 0.9 %copy-start.4 = (f32[256,256]{1,0:T(8,128)S(1)}, f32[256,256]{1,0:T(8,128)}, u32[]{:S(2)}) copy-start(f32[256,256]{1,0:T(8,128)} %constant.41.clone.mf) | copy-start | bytes 786436
  5.9 0.9 %copy-start.5 = (bf16[256,512]{1,0:T(8,128)(2,1)S(1)}, bf16[256,512]{1,0:T(8,128)(2,1)}, u32[]{:S(2)}) copy-start(bf16[256,512]{1,0:T(8,128)(2,1)} %constant.32.clone.r3) | copy-start | bytes 786436
  6.8 0.9 %copy-start.6 = (bf16[128,512]{1,0:T(8,128)(2,1)S(1)}, bf16[128,512]{1,0:T(8,128)(2,1)}, u32[]{:S(2)}) copy-start(bf16[128,512]{1,0:T(8,128)(2,1)} %tok.1) | copy-start | bytes 393220
  7.8 0.9 %copy-start.7 = (f32[256,64]{1,0:T(8,128)S(1)}, f32[256,64]{1,0:T(8,128)}, u32[]{:S(2)}) copy-start(f32[256,64]{1,0:T(8,128)} %constant.38.clone.f1n) | copy-start | bytes 196612
  8.7 0.9 %copy-start.8 = (f32[256,64]{1,0:T(8,128)S(1)}, f32[256,64]{1,0:T(8,128)}, u32[]{:S(2)}) copy-start(f32[256,64]{1,0:T(8,128)} %constant.37.clone.f1p) | copy-start | bytes 196612
  9.6 0.9 %copy-start.9 = (bf16[256,192]{1,0:T(8,128)(2,1)S(1)}, bf16[256,192]{1,0:T(8,128)(2,1)}, u32[]{:S(2)}) copy-start(bf16[256,192]{1,0:T(8,128)(2,1)} %constant.33.clone.r5) | copy-start | bytes 294916
  10.5 0.9 %copy-start.10 = (bf16[256,192]{1,0:T(8,128)(2,1)S(1)}, bf16[256,192]{1,0:T(8,128)(2,1)}, u32[]{:S(2)}) copy-start(bf16[256,192]{1,0:T(8,128)(2,1)} %constant.30.clone.r2q) | copy-start | bytes 294916
  11.4 0.9 copy-start.11
  12.3 0.8 copy-start.12
  13.1 0.8 copy-start.13
  13.9 0.8 copy-start.14
  14.8 0.8 copy-start.15
  15.6 0.8 copy-start.16
  16.5 0.8 copy-start.17
  17.2 0.7 copy-start.18

commit v2 on v1

v2 whole, which is shorter than its diff:
```python
import math

import jax
import jax.numpy as jnp
import numpy as np
from jax import lax
from jax.experimental import pallas as pl
from jax.experimental.pallas import tpu as pltpu
from jax.sharding import PartitionSpec as P

LENGTH = 8192
POINTS = 2 * LENGTH
MESH = pl.DeviceIdType.MESH
F32, BF16 = jnp.float32, jnp.bfloat16
EXACT = lax.Precision.HIGHEST


def selection(outs, ins, pairs):
    matrix = np.zeros((outs, ins), np.float32)
    for row, column in pairs:
        matrix[row, column] = 1.0
    return matrix


def selections():
    def ctx(p, zl):
        return (p >> 1) * 16 + zl * 2 + (p & 1)

    eight = range(8)
    r1 = np.stack([selection(256, 512, [(y * 64 + k, k * 8 + h * 4 + y) for y in range(4) for k in range(64)]) for h in range(2)])
    rg = selection(64, 64, [(y * 16 + h * 8 + n, n * 8 + h * 4 + y) for y in range(4) for h in range(2) for n in eight])
    r2q = selection(256, 192, [(zl * 32 + i * 8 + p, i * 64 + ctx(p, zl)) for zl in eight for i in range(3) for p in eight])
    r2g = np.stack(
        [
            selection(
                256,
                64,
                [
                    (((y % 2) * 4 + n // 2) * 32 + 24 + (own * 2 + y // 2) * 2 + n % 2, y * 16 + h * 8 + n)
                    for y in range(4)
                    for n in eight
                ],
            )
            for own in range(2)
            for h in range(2)
        ]
    )
    r3 = selection(256, 256, [(p * 32 + i * 8 + zl, zl * 32 + i * 8 + p) for zl in eight for i in range(4) for p in eight])
    r5 = selection(192, 192, [(zl * 24 + i * 8 + p, i * 64 + p * 8 + zl) for zl in eight for i in range(3) for p in eight])
    r6 = selection(384, 384, [(p * 48 + z * 3 + i, z * 24 + i * 8 + p) for z in range(16) for i in range(3) for p in eight])
    r8 = selection(
        192,
        192,
        [(zl * 24 + i * 8 + h * 4 + y, y * 48 + h * 24 + zl * 3 + i) for y in range(4) for h in range(2) for zl in eight for i in range(3)],
    )
    r9 = np.stack(
        [
            selection(
                384,
                192,
                [
                    (i * 128 + zl * 16 + c * 8 + h * 4 + y, y * 48 + h * 24 + zl * 3 + i)
                    for y in range(4)
                    for h in range(2)
                    for zl in eight
                    for i in range(3)
                ],
            )
            for c in range(2)
        ]
    )
    return [m.astype(jnp.bfloat16) for m in (r1, rg, r2q, r2g, r3, r5, r6, r8, r9)]


def transforms():
    turn = 2.0 * math.pi
    natural = np.arange(64)
    moved = np.array([(p >> 1) * 16 + zl * 2 + (p & 1) for p in range(8) for zl in range(8)])
    k = np.arange(128)

    def first(rows):
        angle = turn * ((k[:, None] * rows[None, :]) % 128) / 128
        return np.concatenate([np.cos(angle), -np.sin(angle)], 0)

    def last(rows, scale):
        angle = turn * ((rows[:, None] * k[None, :]) % 128) / 128
        return np.concatenate([np.cos(angle), -np.sin(angle)], 1) * scale

    angle = turn * (k[:, None] * k[None, :]) / POINTS
    twist = (np.cos(angle), -np.sin(angle))
    angle = turn * ((k[:, None] * k[None, :]) % 128) / 128
    c, s = np.cos(angle), np.sin(angle)
    forward = np.block([[c, -s], [s, c]])
    back = np.block([[c, s], [-s, c]])
    tables = (
        first(moved),
        first(natural),
        *twist,
        forward,
        back,
        last(moved, 1.0 / POINTS),
        last(natural, 1.0 / (POINTS * math.sqrt(LENGTH))),
    )
    return [t.astype(np.float32) for t in tables]


def dot(left, right, precision=None):
    return jnp.dot(left, right, precision=precision, preferred_element_type=F32)


OPERANDS = [
    "w", "r1", "go", "rg", "r2q", "r2g", "r3", "r5", "r6", "r8", "r9",
    "f1p", "f1n", "twr", "twi", "mf", "mi", "g1p", "g1n",
]


def kernel(tok_in, filt_in, *refs):
    count = len(OPERANDS)
    inputs, refs = refs[:count], refs[count:]
    held, loaded = refs[-count - 1 : -1], refs[-1]
    body(tok_in, filt_in, inputs, held, loaded, *refs[: -count - 1])


def body(
    tok_in, filt_in, inputs, held, loaded,
    ig_out, wg_out, fg_out,
    ig, wg, fg, part, recv1, sendg, recvg, send2, recv2, send3, recv3, send5, recv5, recv6, recv7,
    terms, send8, recv8, toks, turned_w, filt, fg_sent,
    s1, t1, s2, t2, s3, t3, s5, t5, s6, t6, s7, t7, s8, t8, sx, tx, sc, tc, sg, tg, sf, tf, sb, tb, out_sem,
):
    k, j = lax.axis_index("ctx"), lax.axis_index("tp")
    x, zl, core = k // 16, (k // 2) % 8, k % 2
    zh, y = j // 4, j % 4
    z, p = zh * 8 + zl, x * 2 + core

    def at(x_, zl_, core_, zh_, y_):
        return (x_ * 16 + zl_ * 2 + core_, zh_ * 4 + y_)

    def at_y(y_):
        return at(x, zl, core, zh, y_)

    def at_z(z_):
        return at(x, z_ % 8, core, z_ // 8, y)

    def at_p(p_):
        return at(p_ // 2, zl, p_ % 2, zh, y)

    filter_to, filter_from = (j * 8 + k // 8, k % 8), ((k % 8) * 8 + j, k // 8)
    fixed = jnp.logical_and(k == filter_from[0], j == filter_from[1])

    loads = [pltpu.make_async_copy(tok_in, toks.at[p], loaded.at[0])]
    for n, (src, dst) in enumerate(zip(inputs, held)):
        loads.append(pltpu.make_async_copy(src, dst, loaded.at[n + 1]))
    for load in loads[:3]:
        load.start()
    w, r1, go, rg, r2q, r2g, r3, r5, r6, r8, r9, f1p, f1n, twr, twi, mf, mi, g1p, g1n = held
    tok = toks.at[p]

    def need(*names):
        for name in names:
            loads[OPERANDS.index(name) + 1].wait()

    def each(low, high, body):
        def step(n, carry):
            body(n)
            return carry

        lax.fori_loop(low, high, step, 0)

    def send(src, dst, s, t, to):
        pltpu.make_async_remote_copy(
            src_ref=src, dst_ref=dst, send_sem=s, recv_sem=t, device_id=to, device_id_type=MESH
        ).start()

    def take(ref, sem):
        pltpu.make_async_copy(ref, ref, sem).wait()

    owed = {}

    def pay(name):
        owed.pop(name)()

    def finish():
        for name in list(owed):
            pay(name)

    barrier = pltpu.get_barrier_semaphore()

    def greet(to):
        pl.semaphore_signal(barrier, inc=1, device_id=to, device_id_type=MESH)

    each(1, 4, lambda n: greet(at_y((y + n) % 4)))
    each(1, 16, lambda n: greet(at_z((z + n) % 16)))
    each(1, 8, lambda n: greet(at_p((p + n) % 8)))


    @pl.when(jnp.logical_not(fixed))
    def _():
        greet(filter_from)

    for load in loads[3:]:
        load.start()
    loads[0].wait()
    need("w", "r1")

    parts = [dot(tok[...], w[i]).astype(BF16) for i in range(3)]

    def rows_of(h):
        for i in range(3):
            rows = lax.dot_general(r1[h], parts[i], (((1,), (1,)), ((), ())), preferred_element_type=F32).astype(BF16)
            for yy in range(4):
                part[yy, h, i * 64 : i * 64 + 64, :] = rows[yy * 64 : yy * 64 + 64]

    rows_of(1 - zh)
    need("go", "rg")
    sendg[...] = dot(rg[...], go[...]).astype(BF16).reshape(4, 16, 128)
    recvg[y] = sendg[y]

    pl.semaphore_wait(barrier, jnp.where(fixed, 25, 26))
    for n in range(1, 4):
        to = (y + n) % 4
        send(sendg.at[to], recvg.at[y], sg, tg, at_y(to))
    owed["sg"] = lambda: take(recvg.at[pl.ds(0, 3)], sg)
    owed["tg"] = lambda: take(recvg.at[pl.ds(0, 3)], tg)
    for half, h in enumerate((1 - zh, zh)):
        if half == 1:
            rows_of(h)
        for n in range(1, 4):
            to = (y + n) % 4
            send(part.at[to, h], recv1.at[half, n - 1], s1.at[half], t1.at[half], at_y(to))
    for half in range(2):
        owed["t1", half] = lambda half=half: take(recv1.at[half], t1.at[half])
        owed["s1", half] = lambda half=half: take(recv1.at[half], s1.at[half])
    each(1, 4, lambda n: send(tok, toks.at[p], sx, tx, at_p((p + 2 * n) % 8)))
    sibling = x * 2 + (1 - core)
    send(tok, toks.at[p], sc, tc, at_p(sibling))
    owed["tx"] = lambda: take(toks.at[pl.ds(0, 3)], tx)
    owed["sx"] = lambda: take(toks.at[pl.ds(0, 3)], sx)
    owed["tc"] = lambda: take(toks.at[pl.ds(0, 1)], tc)
    owed["sc"] = lambda: take(toks.at[pl.ds(0, 1)], sc)
    def move(src, dst, s, t, to):
        @pl.when(fixed)
        def _():
            pltpu.make_async_copy(src, dst, t).start()

        @pl.when(jnp.logical_not(fixed))
        def _():
            send(src, dst, s, t, to)

    def unless_fixed(ref, sem):
        @pl.when(jnp.logical_not(fixed))
        def _():
            take(ref, sem)

    move(filt_in, filt, sf, tf, filter_to)
    owed["sf"] = lambda: unless_fixed(filt, sf)
    owed["tf"] = lambda: take(filt, tf)
    need(*[name for name in OPERANDS if name not in ("w", "r1", "go", "rg")])

    twist_r, twist_i = twr[...], twi[...]

    def spectrum(table, rows, count):
        a = dot(table[...], rows, EXACT)
        ar, ai = a[:128], a[128:]
        pieces = []
        for n in range(count):
            br, bi = ar[:, n * 128 : n * 128 + 128], ai[:, n * 128 : n * 128 + 128]
            pieces.append(jnp.concatenate([br * twist_r - bi * twist_i, br * twist_i + bi * twist_r], axis=1))
        return dot(jnp.concatenate(pieces, axis=0), mf[...], EXACT)

    def inverse(spectra):
        d = dot(jnp.concatenate(spectra, axis=0), mi[...], EXACT)
        reals, imags = [], []
        for n in range(len(spectra)):
            dr, di = d[n * 128 : n * 128 + 128, :128], d[n * 128 : n * 128 + 128, 128:]
            reals.append(dr * twist_r + di * twist_i)
            imags.append(di * twist_r - dr * twist_i)
        return jnp.concatenate([jnp.concatenate(reals, axis=1), jnp.concatenate(imags, axis=1)], axis=0)

    for b in range(8):
        first = (b // 2) * 128
        wide = jnp.concatenate([w[i, :, first : first + 128] for i in range(3)], axis=1)
        turned_w[b] = dot(wide, r9[b % 2]).astype(BF16)

    def to_z(body):
        def step(n):
            body((z + 8 + (1 - 2 * (n % 2)) * ((n + 1) // 2)) % 16)

        each(0, 15, step)

    def sum_y(half, h):
        pay(("t1", half))
        total = part[y, h].astype(F32)
        for n in range(3):
            total = total + recv1[half, n].astype(F32)
        return total.astype(BF16)

    def slabs(half, h):
        total = sum_y(half, h)
        if half == 0:
            pay("tg")
        cotangent = dot(r2g[zh * 2 + h], recvg[...].reshape(64, 128))
        send2[half] = (dot(r2q[...], total) + cotangent).astype(BF16).reshape(8, 32, 128)

    slabs(0, 1 - zh)

    def to_other(to):
        @pl.when(to // 8 != zh)
        def _():
            send(send2.at[0, to % 8], recv2.at[0, zl], s2.at[0], t2.at[0], at_z(to))

    to_z(to_other)
    owed["t2b"] = lambda: take(recv2.at[0], t2.at[0])
    owed["s2b"] = lambda: take(recv2.at[0], s2.at[0])
    slabs(1, zh)

    def to_own(to):
        @pl.when(to // 8 == zh)
        def _():
            send(send2.at[1, to % 8], recv2.at[1, zl], s2.at[1], t2.at[1], at_z(to))

    to_z(to_own)
    owed["t2a"] = lambda: take(recv2.at[1, pl.ds(0, 7)], t2.at[1])
    owed["s2a"] = lambda: take(recv2.at[1, pl.ds(0, 7)], s2.at[1])
    recv2[1, zl] = send2[1, zl]

    pay("tx")

    def forward(n):
        block = (p + 2 * n) % 8
        send(toks.at[block], toks.at[block], sc, tc, at_p(sibling))

    each(1, 4, forward)
    owed["tc"] = lambda: take(toks.at[pl.ds(0, 4)], tc)
    owed["sc"] = lambda: take(toks.at[pl.ds(0, 4)], sc)

    pay("tf")
    filt_f = spectrum(f1n, filt[...], 1)
    filt_r, filt_i = filt_f[:, :128], filt_f[:, 128:]
    pay("t2a")
    pay("t2b")
    both = recv2[0].astype(F32) + recv2[1].astype(F32)
    moved = dot(r3[...], both.astype(BF16).reshape(256, 128))
    send3[...] = moved.astype(BF16).reshape(8, 32, 128)

    def to_p3(n):
        to = (p + n) % 8
        send(send3.at[to], recv3.at[p], s3, t3, at_p(to))

    each(1, 8, to_p3)
    owed["s3"] = lambda: take(recv3.at[pl.ds(0, 7)], s3)
    owed["t3"] = lambda: take(recv3.at[pl.ds(0, 7)], t3)
    recv3[p] = send3[p]
    pay("t3")

    lines = recv3[...].astype(F32).reshape(8, 4, 8, 128)
    query, key_part, value, cot = [lines[:, i].reshape(64, 128) for i in range(4)]
    spectra = spectrum(f1p, jnp.concatenate([key_part * value, cot * query], axis=1), 2)
    mix_r, mix_i = spectra[:128, :128], spectra[:128, 128:]
    grad_r, grad_i = spectra[128:, :128], spectra[128:, 128:]
    out_f = jnp.concatenate([filt_r * mix_r - filt_i * mix_i, filt_r * mix_i + filt_i * mix_r], axis=1)
    back_f = jnp.concatenate([filt_r * grad_r + filt_i * grad_i, filt_r * grad_i - filt_i * grad_r], axis=1)
    both = dot(g1p[...], inverse([out_f, back_f]), EXACT)
    grad_query = (cot * both[:, :128]).astype(BF16)
    grad_mixed = both[:, 128:].astype(BF16).astype(F32)
    grad_key = (grad_mixed * value).astype(BF16)
    grad_value = (grad_mixed * key_part).astype(BF16)

    rows = jnp.concatenate([grad_query, grad_key, grad_value], axis=0)
    send5[...] = dot(r5[...], rows).reshape(8, 24, 128).astype(BF16)
    to_z(lambda to: send(send5.at[to % 8], recv5.at[z], s5, t5, at_z(to)))
    owed["s5"] = lambda: take(recv5.at[pl.ds(0, 15)], s5)
    owed["t5"] = lambda: take(recv5.at[pl.ds(0, 15)], t5)
    recv5[z] = send5[zl]

    filt_f = jnp.concatenate([mix_r * grad_r + mix_i * grad_i, mix_r * grad_i - mix_i * grad_r], axis=1)
    fg_sent[...] = dot(g1n[...], inverse([filt_f]), EXACT)
    move(fg_sent, fg, sb, tb, filter_from)
    owed["sb"] = lambda: unless_fixed(fg, sb)
    owed["tb"] = lambda: take(fg, tb)
    outs = [pltpu.make_async_copy(src, dst, out_sem.at[n]) for n, (src, dst) in enumerate(((fg, fg_out), (ig, ig_out), (wg, wg_out)))]

    pay("t5")
    moved = dot(r6[...], recv5[...].astype(F32).reshape(384, 128).astype(BF16))
    recv6[y] = moved.astype(BF16).reshape(8, 48, 128)
    for n in range(1, 4):
        send(recv6.at[y], recv6.at[y], s6, t6.at[4 - n], at_y((y + n) % 4))
        owed["t6", n] = lambda n=n: take(recv6.at[(y + n) % 4], t6.at[n])
    owed["s6"] = lambda: take(recv6.at[pl.ds(0, 3)], s6)

    pay("tc")
    for n in (0, 1, 3, 2):
        yy = (y + n) % 4
        if n > 0:
            pay(("t6", n))
        wide = jnp.concatenate([recv6[yy, b] for b in range(8)], axis=1)
        terms[yy] = dot(wide, toks[...].reshape(1024, 512)).astype(BF16)
        if n == 2:
            moved = dot(r8[...], terms[...].reshape(192, 512))
            send8[...] = moved.reshape(8, 24, 512).astype(BF16)

            def to_8(r):
                to = (zl + 4 + (1 - 2 * (r % 2)) * ((r + 1) // 2)) % 8
                send(send8.at[to], recv8.at[zl], s8, t8, at(x, to, core, zh, y))

            each(0, 7, to_8)
            recv8[zl] = send8[zl]

        def to_p7(r, yy=yy):
            to = (p + r) % 8
            send(recv6.at[yy, to], recv7.at[p, yy], s7, t7, at_p(to))

        each(1, 8, to_p7)
        recv7[p, yy] = recv6[yy, p]

    owed["s7"] = lambda: take(recv7.at[pl.ds(0, 7)], s7)
    owed["t7"] = lambda: take(recv7.at[pl.ds(0, 7)], t7)
    owed["s8"] = lambda: take(recv8.at[pl.ds(0, 7)], s8)
    owed["t8"] = lambda: take(recv8.at[pl.ds(0, 7)], t8)
    pay("tb")
    outs[0].start()

    pay("t7")
    total = dot(turned_w[0], recv7[0].reshape(192, 128))
    for b in range(1, 8):
        total = total + dot(turned_w[b], recv7[b].reshape(192, 128))
    ig[...] = total.T.astype(BF16)
    outs[1].start()

    pay("t8")
    total = recv8[0].astype(F32)
    for n in range(1, 8):
        total = total + recv8[n].astype(F32)
    wg[...] = (total * (1.0 / math.sqrt(LENGTH))).reshape(3, 8, 512)
    outs[2].start()

    finish()
    for out in outs:
        out.wait()


def hand_over(*refs):
    sources, results, held, sems = refs[:3], refs[3:6], refs[6:9], refs[9]
    first = [pltpu.make_async_copy(src, dst, sems.at[n]) for n, (src, dst) in enumerate(zip(sources, held))]
    then = [pltpu.make_async_copy(src, dst, sems.at[3 + n]) for n, (src, dst) in enumerate(zip(held, results))]
    for copy in first:
        copy.start()
    for before, copy in zip(first, then):
        before.wait()
        copy.start()
    for copy in then:
        copy.wait()


def on_device(tokens, w_in, grad_out, filters):
    tables = [jnp.asarray(t) for t in selections()] + [jnp.asarray(t) for t in transforms()]
    r1, rg, *rest = tables
    operands = [w_in.transpose(1, 0, 2), r1, grad_out.T, rg, *rest]
    vmem = pl.BlockSpec(memory_space=pltpu.VMEM)
    hbm = pl.BlockSpec(memory_space=pltpu.HBM)
    dma = pltpu.SemaphoreType.DMA
    shapes = (
        jax.ShapeDtypeStruct((128, 512), BF16),
        jax.ShapeDtypeStruct((3, 8, 512), F32),
        jax.ShapeDtypeStruct((64, 128), F32),
    )
    made = pl.pallas_call(
        kernel,
        out_shape=shapes,
        in_specs=[hbm] * (2 + len(operands)),
        out_specs=(hbm, hbm, hbm),
        scratch_shapes=[
            *[pltpu.VMEM(a.shape, a.dtype) for a in shapes],
            pltpu.VMEM((4, 2, 192, 128), BF16),
            pltpu.VMEM((2, 3, 192, 128), BF16),
            pltpu.VMEM((4, 16, 128), BF16),
            pltpu.VMEM((4, 16, 128), BF16),
            pltpu.VMEM((2, 8, 32, 128), BF16),
            pltpu.VMEM((2, 8, 32, 128), BF16),
            pltpu.VMEM((8, 32, 128), BF16),
            pltpu.VMEM((8, 32, 128), BF16),
            pltpu.VMEM((8, 24, 128), BF16),
            pltpu.VMEM((16, 24, 128), BF16),
            pltpu.VMEM((4, 8, 48, 128), BF16),
            pltpu.VMEM((8, 4, 48, 128), BF16),
            pltpu.VMEM((4, 48, 512), BF16),
            pltpu.VMEM((8, 24, 512), BF16),
            pltpu.VMEM((8, 24, 512), BF16),
            pltpu.VMEM((8, 128, 512), BF16),
            pltpu.VMEM((8, 512, 192), BF16),
            pltpu.VMEM((64, 128), F32),
            pltpu.VMEM((64, 128), F32),
            dma((2,)), dma((2,)), dma((2,)), dma((2,)),
            dma, dma, dma, dma,
            dma, dma((4,)),
            dma, dma, dma, dma,
            dma, dma, dma, dma,
            dma, dma, dma, dma, dma, dma,
            dma((3,)),
            *[pltpu.VMEM(a.shape, a.dtype) for a in operands],
            dma((1 + len(operands),)),
        ],
        compiler_params=pltpu.CompilerParams(collective_id=0, has_side_effects=True, vmem_limit_bytes=63 * 1024 * 1024),
    )(tokens, filters.reshape(64, 128), *operands)
    input_grad, weight_grad, filter_grad = pl.pallas_call(
        hand_over,
        out_shape=shapes,
        in_specs=[hbm] * 3,
        out_specs=(hbm, hbm, hbm),
        scratch_shapes=[*[pltpu.VMEM(a.shape, a.dtype) for a in shapes], dma((6,))],
        compiler_params=pltpu.CompilerParams(vmem_limit_bytes=63 * 1024 * 1024),
    )(*made)
    return input_grad, weight_grad.transpose(1, 0, 2), filter_grad.reshape(1, 1, LENGTH)


def solution(mesh):
    placed = (P("ctx", "tp"), P("tp", None, None), P("ctx", "tp"), P("tp", "ctx", None))
    return jax.shard_map(
        on_device,
        mesh=mesh,
        in_specs=placed,
        out_specs=(P("ctx", "tp"), P("ctx", None, "tp"), P("tp", "ctx", None)),
        check_vma=False,
    )
```

time: 91.2 us -> 66 us (0.72)
  the two profiles are of different devices: /device:TPU:31 before, /device:TPU:24 now
where the time goes in v2:
time: 66 us; the launch traced here: 65.4 us
  Pallas kernels  64.8 us (98%)
    pallas_call x1, Pallas kernels, on_device(): pl.pallas_call(kernel, out_shape=shapes, in_specs=[hbm] * (2 + len(operan...  63.1 us
    pallas_call x1, Pallas kernels, on_device(): pl.pallas_call(hand_over, out_shape=shapes, in_specs=[hbm] * 3, out_specs...  1.63 us

profile of v2, /device:TPU:24, one launch (start us, length us, event | category | flops | bytes accessed | tf_op | source)
XLA Modules:
  0.0 65.4 jit_solution(5702485609042578608)
XLA Ops:
  0.6 63.1 %shard_map.220 = (bf16[128,512]{1,0:T(8,128)(2,1)}, f32[3,8,512]{2,1,0:T(8,128)}, f32[64,128]{1,0:T(8,128)}) custom-call(bf16[128,512]{1,0:T(8,128)(2,1)} %tok_in.1, f32[64,128]{1,0:T(8,128)} %bitcast.6, bf16[3,512,512]{2,1,0:T(8,128)(2,1)} %bitcast.5, bf16[2,256,512]{2,1,0:T(8,128)(2,1)} %constant.34.clone.refs_1_, bf16[64,128]{1,0:T(8,128)(2,1)} %bitcast.7, ...), custom_call_target="tpu_custom_call" | custom-call | tf_op jit(solution)/shard_map/pallas_call | solution.py:467
  63.8 1.6 %shard_map.221 = (bf16[128,512]{1,0:T(8,128)(2,1)}, f32[3,8,512]{2,1,0:T(8,128)}, f32[64,128]{1,0:T(8,128)}) custom-call(bf16[128,512]{1,0:T(8,128)(2,1)} %get-tuple-element.9.refs_0_, f32[3,8,512]{2,1,0:T(8,128)} %get-tuple-element.10.refs_1_, f32[64,128]{1,0:T(8,128)} %get-tuple-element.11.refs_2_), custom_call_target="tpu_custom_call" | custom-call | tf_op jit(solution)/shard_map/pallas_call | solution.py:505

commit v3 on v2

--- a/solution.py
+++ b/solution.py
@@ -12,7 +12,6 @@
 POINTS = 2 * LENGTH
 MESH = pl.DeviceIdType.MESH
 F32, BF16 = jnp.float32, jnp.bfloat16
-EXACT = lax.Precision.HIGHEST
 
 
 def selection(outs, ins, pairs):
@@ -51,7 +50,7 @@
     r8 = selection(
         192,
         192,
-        [(zl * 24 + i * 8 + h * 4 + y, y * 48 + h * 24 + zl * 3 + i) for y in range(4) for h in range(2) for zl in eight for i in range(3)],
+        [(zl * 24 + q * 6 + h * 3 + i, q * 48 + h * 24 + zl * 3 + i) for q in range(4) for h in range(2) for zl in eight for i in range(3)],
     )
     r9 = np.stack(
         [
@@ -101,11 +100,24 @@
         last(moved, 1.0 / POINTS),
         last(natural, 1.0 / (POINTS * math.sqrt(LENGTH))),
     )
-    return [t.astype(np.float32) for t in tables]
-
-
-def dot(left, right, precision=None):
-    return jnp.dot(left, right, precision=precision, preferred_element_type=F32)
+    axes = (1, 1, None, None, 0, 0, 1, 1)
+    return [t.astype(np.float32) if a is None else pieces_of_table(t, a) for t, a in zip(tables, axes)]
+
+
+def pieces_of_table(table, axis):
+    high = table.astype(jnp.bfloat16)
+    low = (table - high.astype(np.float64)).astype(jnp.bfloat16)
+    return np.concatenate([high, high, low], axis=axis)
+
+
+def pieces_of(values, axis):
+    high = values.astype(BF16)
+    low = (values - high.astype(F32)).astype(BF16)
+    return jnp.concatenate([high, low, high], axis=axis)
+
+
+def dot(left, right):
+    return jnp.dot(left, right, preferred_element_type=F32)
 
 
 OPERANDS = [
@@ -125,7 +137,7 @@
     tok_in, filt_in, inputs, held, loaded,
     ig_out, wg_out, fg_out,
     ig, wg, fg, part, recv1, sendg, recvg, send2, recv2, send3, recv3, send5, recv5, recv6, recv7,
-    terms, send8, recv8, toks, turned_w, filt, fg_sent,
+    send8, recv8, toks, turned_w, filt, fg_sent,
     s1, t1, s2, t2, s3, t3, s5, t5, s6, t6, s7, t7, s8, t8, sx, tx, sc, tc, sg, tg, sf, tf, sb, tb, out_sem,
 ):
     k, j = lax.axis_index("ctx"), lax.axis_index("tp")
@@ -260,16 +272,16 @@
     twist_r, twist_i = twr[...], twi[...]
 
     def spectrum(table, rows, count):
-        a = dot(table[...], rows, EXACT)
+        a = dot(table[...], pieces_of(rows, 0))
         ar, ai = a[:128], a[128:]
         pieces = []
         for n in range(count):
             br, bi = ar[:, n * 128 : n * 128 + 128], ai[:, n * 128 : n * 128 + 128]
             pieces.append(jnp.concatenate([br * twist_r - bi * twist_i, br * twist_i + bi * twist_r], axis=1))
-        return dot(jnp.concatenate(pieces, axis=0), mf[...], EXACT)
+        return dot(pieces_of(jnp.concatenate(pieces, axis=0), 1), mf[...])
 
     def inverse(spectra):
-        d = dot(jnp.concatenate(spectra, axis=0), mi[...], EXACT)
+        d = dot(pieces_of(jnp.concatenate(spectra, axis=0), 1), mi[...])
         reals, imags = [], []
         for n in range(len(spectra)):
             dr, di = d[n * 128 : n * 128 + 128, :128], d[n * 128 : n * 128 + 128, 128:]
@@ -277,11 +289,6 @@
             imags.append(di * twist_r - dr * twist_i)
         return jnp.concatenate([jnp.concatenate(reals, axis=1), jnp.concatenate(imags, axis=1)], axis=0)
 
-    for b in range(8):
-        first = (b // 2) * 128
-        wide = jnp.concatenate([w[i, :, first : first + 128] for i in range(3)], axis=1)
-        turned_w[b] = dot(wide, r9[b % 2]).astype(BF16)
-
     def to_z(body):
         def step(n):
             body((z + 8 + (1 - 2 * (n % 2)) * ((n + 1) // 2)) % 16)
@@ -324,19 +331,6 @@
     owed["s2a"] = lambda: take(recv2.at[1, pl.ds(0, 7)], s2.at[1])
     recv2[1, zl] = send2[1, zl]
 
-    pay("tx")
-
-    def forward(n):
-        block = (p + 2 * n) % 8
-        send(toks.at[block], toks.at[block], sc, tc, at_p(sibling))
-
-    each(1, 4, forward)
-    owed["tc"] = lambda: take(toks.at[pl.ds(0, 4)], tc)
-    owed["sc"] = lambda: take(toks.at[pl.ds(0, 4)], sc)
-
-    pay("tf")
-    filt_f = spectrum(f1n, filt[...], 1)
-    filt_r, filt_i = filt_f[:, :128], filt_f[:, 128:]
     pay("t2a")
     pay("t2b")
     both = recv2[0].astype(F32) + recv2[1].astype(F32)
@@ -351,6 +345,19 @@
     owed["s3"] = lambda: take(recv3.at[pl.ds(0, 7)], s3)
     owed["t3"] = lambda: take(recv3.at[pl.ds(0, 7)], t3)
     recv3[p] = send3[p]
+    pay("tx")
+
+    def forward(n):
+        block = (p + 2 * n) % 8
+        send(toks.at[block], toks.at[block], sc, tc, at_p(sibling))
+
+    each(1, 4, forward)
+    owed["tc"] = lambda: take(toks.at[pl.ds(0, 4)], tc)
+    owed["sc"] = lambda: take(toks.at[pl.ds(0, 4)], sc)
+
+    pay("tf")
+    filt_f = spectrum(f1n, filt[...], 1)
+    filt_r, filt_i = filt_f[:, :128], filt_f[:, 128:]
     pay("t3")
 
     lines = recv3[...].astype(F32).reshape(8, 4, 8, 128)
@@ -360,7 +367,7 @@
     grad_r, grad_i = spectra[128:, :128], spectra[128:, 128:]
     out_f = jnp.concatenate([filt_r * mix_r - filt_i * mix_i, filt_r * mix_i + filt_i * mix_r], axis=1)
     back_f = jnp.concatenate([filt_r * grad_r + filt_i * grad_i, filt_r * grad_i - filt_i * grad_r], axis=1)
-    both = dot(g1p[...], inverse([out_f, back_f]), EXACT)
+    both = dot(g1p[...], pieces_of(inverse([out_f, back_f]), 0))
     grad_query = (cot * both[:, :128]).astype(BF16)
     grad_mixed = both[:, 128:].astype(BF16).astype(F32)
     grad_key = (grad_mixed * value).astype(BF16)
@@ -374,44 +381,62 @@
     recv5[z] = send5[zl]
 
     filt_f = jnp.concatenate([mix_r * grad_r + mix_i * grad_i, mix_r * grad_i - mix_i * grad_r], axis=1)
-    fg_sent[...] = dot(g1n[...], inverse([filt_f]), EXACT)
+    fg_sent[...] = dot(g1n[...], pieces_of(inverse([filt_f]), 0))
     move(fg_sent, fg, sb, tb, filter_from)
     owed["sb"] = lambda: unless_fixed(fg, sb)
     owed["tb"] = lambda: take(fg, tb)
     outs = [pltpu.make_async_copy(src, dst, out_sem.at[n]) for n, (src, dst) in enumerate(((fg, fg_out), (ig, ig_out), (wg, wg_out)))]
 
+    for b in range(8):
+        first = (b // 2) * 128
+        wide = jnp.concatenate([w[i, :, first : first + 128] for i in range(3)], axis=1)
+        turned_w[b] = dot(wide, r9[b % 2]).astype(BF16)
+
     pay("t5")
     moved = dot(r6[...], recv5[...].astype(F32).reshape(384, 128).astype(BF16))
     recv6[y] = moved.astype(BF16).reshape(8, 48, 128)
-    for n in range(1, 4):
+    for n in (1, 3, 2):
         send(recv6.at[y], recv6.at[y], s6, t6.at[4 - n], at_y((y + n) % 4))
         owed["t6", n] = lambda n=n: take(recv6.at[(y + n) % 4], t6.at[n])
     owed["s6"] = lambda: take(recv6.at[pl.ds(0, 3)], s6)
 
-    pay("tc")
-    for n in (0, 1, 3, 2):
-        yy = (y + n) % 4
-        if n > 0:
-            pay(("t6", n))
-        wide = jnp.concatenate([recv6[yy, b] for b in range(8)], axis=1)
-        terms[yy] = dot(wide, toks[...].reshape(1024, 512)).astype(BF16)
-        if n == 2:
-            moved = dot(r8[...], terms[...].reshape(192, 512))
-            send8[...] = moved.reshape(8, 24, 512).astype(BF16)
-
-            def to_8(r):
-                to = (zl + 4 + (1 - 2 * (r % 2)) * ((r + 1) // 2)) % 8
-                send(send8.at[to], recv8.at[zl], s8, t8, at(x, to, core, zh, y))
-
-            each(0, 7, to_8)
-            recv8[zl] = send8[zl]
-
-        def to_p7(r, yy=yy):
+    def far_first_8(body):
+        def step(n):
+            to = zl + (1 - 2 * (n % 2)) * (7 - n // 2)
+
+            @pl.when(jnp.logical_and(to >= 0, to < 8))
+            def _():
+                body(to)
+
+        each(0, 14, step)
+
+    def weight_terms(those):
+        wide = [jnp.concatenate([recv6[yy, b] for b in range(8)], axis=1) for yy in those]
+        term = dot(jnp.concatenate(wide, axis=0), toks[...].reshape(1024, 512)).astype(BF16)
+        for n, yy in enumerate(those):
+            tall = jnp.concatenate([term[n * 48 : n * 48 + 48, q * 128 : q * 128 + 128] for q in range(4)], axis=0)
+            send8[yy] = dot(r8[...], tall).reshape(8, 24, 128).astype(BF16)
+            far_first_8(lambda to, yy=yy: send(send8.at[yy, to], recv8.at[zl, yy], s8, t8, at(x, to, core, zh, y)))
+            recv8[zl, yy] = send8[yy, zl]
+
+    def to_owners(yy):
+        def to_p7(r):
             to = (p + r) % 8
             send(recv6.at[yy, to], recv7.at[p, yy], s7, t7, at_p(to))
 
         each(1, 8, to_p7)
         recv7[p, yy] = recv6[yy, p]
+
+    pay("tc")
+    weight_terms([y])
+    to_owners(y)
+    pay(("t6", 1))
+    pay(("t6", 3))
+    weight_terms([(y + 1) % 4, (y + 3) % 4])
+    pay(("t6", 2))
+    weight_terms([(y + 2) % 4])
+    for n in (1, 3, 2):
+        to_owners((y + n) % 4)
 
     owed["s7"] = lambda: take(recv7.at[pl.ds(0, 7)], s7)
     owed["t7"] = lambda: take(recv7.at[pl.ds(0, 7)], t7)
@@ -431,7 +456,13 @@
     total = recv8[0].astype(F32)
     for n in range(1, 8):
         total = total + recv8[n].astype(F32)
-    wg[...] = (total * (1.0 / math.sqrt(LENGTH))).reshape(3, 8, 512)
+    total = total * (1.0 / math.sqrt(LENGTH))
+    for yy in range(4):
+        for q in range(4):
+            for h in range(2):
+                for i in range(3):
+                    row = q * 6 + h * 3 + i
+                    wg[i, h * 4 + yy : h * 4 + yy + 1, q * 128 : q * 128 + 128] = total[yy, row : row + 1]
     outs[2].start()
 
     finish()
@@ -483,9 +514,8 @@
             pltpu.VMEM((16, 24, 128), BF16),
             pltpu.VMEM((4, 8, 48, 128), BF16),
             pltpu.VMEM((8, 4, 48, 128), BF16),
-            pltpu.VMEM((4, 48, 512), BF16),
-            pltpu.VMEM((8, 24, 512), BF16),
-            pltpu.VMEM((8, 24, 512), BF16),
+            pltpu.VMEM((4, 8, 24, 128), BF16),
+            pltpu.VMEM((8, 4, 24, 128), BF16),
             pltpu.VMEM((8, 128, 512), BF16),
             pltpu.VMEM((8, 512, 192), BF16),
             pltpu.VMEM((64, 128), F32),

time: 66 us -> 63.4 us (0.961)
  Pallas kernels: 64.8 us -> 62.6 us
    pallas_call x1, Pallas kernels: 63.1 us -> 61 us  [on_device(): pl.pallas_call(kernel, out_shape=shapes, in_specs=[hbm] * (2 + len(operan...]
where the time goes in v3:
time: 63.4 us; the launch traced here: 63.2 us
  Pallas kernels  62.6 us (99%)
  between operations  0.64 us (1%)
    pallas_call x1, Pallas kernels, on_device(): pl.pallas_call(kernel, out_shape=shapes, in_specs=[hbm] * (2 + len(operan...  61 us
    pallas_call x1, Pallas kernels, on_device(): pl.pallas_call(hand_over, out_shape=shapes, in_specs=[hbm] * 3, out_specs...  1.63 us

profile of v3, /device:TPU:24, one launch (start us, length us, event | category | flops | bytes accessed | tf_op | source)
XLA Modules:
  0.0 63.2 jit_solution(3781665634300863222)
XLA Ops:
  0.6 61.0 %shard_map.220 = (bf16[128,512]{1,0:T(8,128)(2,1)}, f32[3,8,512]{2,1,0:T(8,128)}, f32[64,128]{1,0:T(8,128)}) custom-call(bf16[128,512]{1,0:T(8,128)(2,1)} %tok_in.1, f32[64,128]{1,0:T(8,128)} %bitcast.6, bf16[3,512,512]{2,1,0:T(8,128)(2,1)} %bitcast.5, bf16[2,256,512]{2,1,0:T(8,128)(2,1)} %constant.34.clone.refs_1_, bf16[64,128]{1,0:T(8,128)(2,1)} %bitcast.7, ...), custom_call_target="tpu_custom_call" | custom-call | tf_op jit(solution)/shard_map/pallas_call | solution.py:498
  61.6 1.6 %shard_map.221 = (bf16[128,512]{1,0:T(8,128)(2,1)}, f32[3,8,512]{2,1,0:T(8,128)}, f32[64,128]{1,0:T(8,128)}) custom-call(bf16[128,512]{1,0:T(8,128)(2,1)} %get-tuple-element.9.refs_0_, f32[3,8,512]{2,1,0:T(8,128)} %get-tuple-element.10.refs_1_, f32[64,128]{1,0:T(8,128)} %get-tuple-element.11.refs_2_), custom_call_target="tpu_custom_call" | custom-call | tf_op jit(solution)/shard_map/pallas_call | solution.py:535

commit v4 on v3

--- a/solution.py
+++ b/solution.py
@@ -52,7 +52,7 @@
         192,
         [(zl * 24 + q * 6 + h * 3 + i, q * 48 + h * 24 + zl * 3 + i) for q in range(4) for h in range(2) for zl in eight for i in range(3)],
     )
-    r9 = np.stack(
+    r9 = np.concatenate(
         [
             selection(
                 384,
@@ -66,7 +66,8 @@
                 ],
             )
             for c in range(2)
-        ]
+        ],
+        axis=1,
     )
     return [m.astype(jnp.bfloat16) for m in (r1, rg, r2q, r2g, r3, r5, r6, r8, r9)]
 
@@ -201,15 +202,19 @@
     def greet(to):
         pl.semaphore_signal(barrier, inc=1, device_id=to, device_id_type=MESH)
 
+    def far_first_16(body):
+        def step(n):
+            body((z + 8 + (1 - 2 * (n % 2)) * ((n + 1) // 2)) % 16)
+
+        each(0, 15, step)
+
     each(1, 4, lambda n: greet(at_y((y + n) % 4)))
-    each(1, 16, lambda n: greet(at_z((z + n) % 16)))
-    each(1, 8, lambda n: greet(at_p((p + n) % 8)))
-
-
     @pl.when(jnp.logical_not(fixed))
     def _():
         greet(filter_from)
 
+    each(1, 16, lambda n: greet(at_z((z + n) % 16)))
+    each(1, 8, lambda n: greet(at_p((p + n) % 8)))
     for load in loads[3:]:
         load.start()
     loads[0].wait()
@@ -289,12 +294,6 @@
             imags.append(di * twist_r - dr * twist_i)
         return jnp.concatenate([jnp.concatenate(reals, axis=1), jnp.concatenate(imags, axis=1)], axis=0)
 
-    def to_z(body):
-        def step(n):
-            body((z + 8 + (1 - 2 * (n % 2)) * ((n + 1) // 2)) % 16)
-
-        each(0, 15, step)
-
     def sum_y(half, h):
         pay(("t1", half))
         total = part[y, h].astype(F32)
@@ -316,7 +315,7 @@
         def _():
             send(send2.at[0, to % 8], recv2.at[0, zl], s2.at[0], t2.at[0], at_z(to))
 
-    to_z(to_other)
+    far_first_16(to_other)
     owed["t2b"] = lambda: take(recv2.at[0], t2.at[0])
     owed["s2b"] = lambda: take(recv2.at[0], s2.at[0])
     slabs(1, zh)
@@ -326,7 +325,7 @@
         def _():
             send(send2.at[1, to % 8], recv2.at[1, zl], s2.at[1], t2.at[1], at_z(to))
 
-    to_z(to_own)
+    far_first_16(to_own)
     owed["t2a"] = lambda: take(recv2.at[1, pl.ds(0, 7)], t2.at[1])
     owed["s2a"] = lambda: take(recv2.at[1, pl.ds(0, 7)], s2.at[1])
     recv2[1, zl] = send2[1, zl]
@@ -375,7 +374,7 @@
 
     rows = jnp.concatenate([grad_query, grad_key, grad_value], axis=0)
     send5[...] = dot(r5[...], rows).reshape(8, 24, 128).astype(BF16)
-    to_z(lambda to: send(send5.at[to % 8], recv5.at[z], s5, t5, at_z(to)))
+    far_first_16(lambda to: send(send5.at[to % 8], recv5.at[z], s5, t5, at_z(to)))
     owed["s5"] = lambda: take(recv5.at[pl.ds(0, 15)], s5)
     owed["t5"] = lambda: take(recv5.at[pl.ds(0, 15)], t5)
     recv5[z] = send5[zl]
@@ -387,10 +386,9 @@
     owed["tb"] = lambda: take(fg, tb)
     outs = [pltpu.make_async_copy(src, dst, out_sem.at[n]) for n, (src, dst) in enumerate(((fg, fg_out), (ig, ig_out), (wg, wg_out)))]
 
-    for b in range(8):
-        first = (b // 2) * 128
-        wide = jnp.concatenate([w[i, :, first : first + 128] for i in range(3)], axis=1)
-        turned_w[b] = dot(wide, r9[b % 2]).astype(BF16)
+    for b in range(4):
+        wide = jnp.concatenate([w[i, :, b * 128 : b * 128 + 128] for i in range(3)], axis=1)
+        turned_w[:, b * 384 : b * 384 + 384] = dot(wide, r9[...]).astype(BF16)
 
     pay("t5")
     moved = dot(r6[...], recv5[...].astype(F32).reshape(384, 128).astype(BF16))
@@ -433,10 +431,11 @@
     pay(("t6", 1))
     pay(("t6", 3))
     weight_terms([(y + 1) % 4, (y + 3) % 4])
+    to_owners((y + 1) % 4)
+    to_owners((y + 3) % 4)
     pay(("t6", 2))
     weight_terms([(y + 2) % 4])
-    for n in (1, 3, 2):
-        to_owners((y + n) % 4)
+    to_owners((y + 2) % 4)
 
     owed["s7"] = lambda: take(recv7.at[pl.ds(0, 7)], s7)
     owed["t7"] = lambda: take(recv7.at[pl.ds(0, 7)], t7)
@@ -446,9 +445,7 @@
     outs[0].start()
 
     pay("t7")
-    total = dot(turned_w[0], recv7[0].reshape(192, 128))
-    for b in range(1, 8):
-        total = total + dot(turned_w[b], recv7[b].reshape(192, 128))
+    total = dot(turned_w[...], recv7[...].reshape(1536, 128))
     ig[...] = total.T.astype(BF16)
     outs[1].start()
 
@@ -517,7 +514,7 @@
             pltpu.VMEM((4, 8, 24, 128), BF16),
             pltpu.VMEM((8, 4, 24, 128), BF16),
             pltpu.VMEM((8, 128, 512), BF16),
-            pltpu.VMEM((8, 512, 192), BF16),
+            pltpu.VMEM((512, 1536), BF16),
             pltpu.VMEM((64, 128), F32),
             pltpu.VMEM((64, 128), F32),
             dma((2,)), dma((2,)), dma((2,)), dma((2,)),

time: 63.4 us -> 63 us (level)
  no operation moved by 1% of the time
where the time goes in v4:
time: 63 us; the launch traced here: 62.9 us
  Pallas kernels  62.2 us (99%)
  between operations  0.64 us (1%)
    pallas_call x1, Pallas kernels, on_device(): pl.pallas_call(kernel, out_shape=shapes, in_specs=[hbm] * (2 + len(operan...  60.6 us
    pallas_call x1, Pallas kernels, on_device(): pl.pallas_call(hand_over, out_shape=shapes, in_specs=[hbm] * 3, out_specs...  1.63 us

profile of v4, /device:TPU:24, one launch (start us, length us, event | category | flops | bytes accessed | tf_op | source)
XLA Modules:
  0.0 62.9 jit_solution(17503678234426343711)
XLA Ops:
  0.6 60.6 %shard_map.220 = (bf16[128,512]{1,0:T(8,128)(2,1)}, f32[3,8,512]{2,1,0:T(8,128)}, f32[64,128]{1,0:T(8,128)}) custom-call(bf16[128,512]{1,0:T(8,128)(2,1)} %tok_in.1, f32[64,128]{1,0:T(8,128)} %bitcast.6, bf16[3,512,512]{2,1,0:T(8,128)(2,1)} %bitcast.5, bf16[2,256,512]{2,1,0:T(8,128)(2,1)} %constant.34.clone.refs_1_, bf16[64,128]{1,0:T(8,128)(2,1)} %bitcast.7, ...), custom_call_target="tpu_custom_call" | custom-call | tf_op jit(solution)/shard_map/pallas_call | solution.py:495
  61.3 1.6 %shard_map.221 = (bf16[128,512]{1,0:T(8,128)(2,1)}, f32[3,8,512]{2,1,0:T(8,128)}, f32[64,128]{1,0:T(8,128)}) custom-call(bf16[128,512]{1,0:T(8,128)(2,1)} %get-tuple-element.9.refs_0_, f32[3,8,512]{2,1,0:T(8,128)} %get-tuple-element.10.refs_1_, f32[64,128]{1,0:T(8,128)} %get-tuple-element.11.refs_2_), custom_call_target="tpu_custom_call" | custom-call | tf_op jit(solution)/shard_map/pallas_call | solution.py:532

commit v5 on v3

--- a/solution.py
+++ b/solution.py
@@ -442,8 +442,6 @@
     owed["t7"] = lambda: take(recv7.at[pl.ds(0, 7)], t7)
     owed["s8"] = lambda: take(recv8.at[pl.ds(0, 7)], s8)
     owed["t8"] = lambda: take(recv8.at[pl.ds(0, 7)], t8)
-    pay("tb")
-    outs[0].start()
 
     pay("t7")
     total = dot(turned_w[0], recv7[0].reshape(192, 128))
@@ -451,6 +449,8 @@
         total = total + dot(turned_w[b], recv7[b].reshape(192, 128))
     ig[...] = total.T.astype(BF16)
     outs[1].start()
+    pay("tb")
+    outs[0].start()
 
     pay("t8")
     total = recv8[0].astype(F32)

time: 63.4 us -> 63.4 us (level)
  no operation moved by 1% of the time
where the time goes in v5:
time: 63.4 us; the launch traced here: 63.2 us
  Pallas kernels  62.6 us (99%)
  between operations  0.64 us (1%)
    pallas_call x1, Pallas kernels, on_device(): pl.pallas_call(kernel, out_shape=shapes, in_specs=[hbm] * (2 + len(operan...  61 us
    pallas_call x1, Pallas kernels, on_device(): pl.pallas_call(hand_over, out_shape=shapes, in_specs=[hbm] * 3, out_specs...  1.63 us

profile of v5, /device:TPU:24, one launch (start us, length us, event | category | flops | bytes accessed | tf_op | source)
XLA Modules:
  0.0 63.2 jit_solution(7806586886948334460)
XLA Ops:
  0.6 61.0 %shard_map.220 = (bf16[128,512]{1,0:T(8,128)(2,1)}, f32[3,8,512]{2,1,0:T(8,128)}, f32[64,128]{1,0:T(8,128)}) custom-call(bf16[128,512]{1,0:T(8,128)(2,1)} %tok_in.1, f32[64,128]{1,0:T(8,128)} %bitcast.6, bf16[3,512,512]{2,1,0:T(8,128)(2,1)} %bitcast.5, bf16[2,256,512]{2,1,0:T(8,128)(2,1)} %constant.34.clone.refs_1_, bf16[64,128]{1,0:T(8,128)(2,1)} %bitcast.7, ...), custom_call_target="tpu_custom_call" | custom-call | tf_op jit(solution)/shard_map/pallas_call | solution.py:498
  61.6 1.6 %shard_map.221 = (bf16[128,512]{1,0:T(8,128)(2,1)}, f32[3,8,512]{2,1,0:T(8,128)}, f32[64,128]{1,0:T(8,128)}) custom-call(bf16[128,512]{1,0:T(8,128)(2,1)} %get-tuple-element.9.refs_0_, f32[3,8,512]{2,1,0:T(8,128)} %get-tuple-element.10.refs_1_, f32[64,128]{1,0:T(8,128)} %get-tuple-element.11.refs_2_), custom_call_target="tpu_custom_call" | custom-call | tf_op jit(solution)/shard_map/pallas_call | solution.py:535
